TPU v7x, 32 devices: a whole 2x2x4 slice. The times are simulated.
32 devices in a mesh: groups: 2 (over y), seq: 4 (over z), chan: 4 (over x, core).
Axes of the slice: x: 2, y: 2, z: 4, core: 2. Of those that a mesh axis runs over, the one named last changes fastest.
Arguments:
- tokens: bfloat16 [8, 2, 128, 4096], P(('groups', 'seq'), None, None, 'chan'), parts along dimension 0, may hold values from -6 to 6
- w_up: bfloat16 [4096, 4096], P(None, 'chan'), may hold values from -0.09375 to 0.09375
- w_out: bfloat16 [4096, 4096], P('chan'), may hold values from -0.09375 to 0.09375
- rpe_in_w: float32 [64], replicated, may hold values from -1 to 128
- rpe_in_b: float32 [64], replicated, may hold values from -128 to 2
- rpe_mid_w: float32 [64, 64], replicated, may hold values from -32 to 32
- rpe_out_w: float32 [64, 2048], replicated, may hold values from -0.75 to 0.75
- decay_rate: float32 [2048], replicated, may hold values from 0.00029296876 to 0.05
- conv_taps: float32 [5, 2048], replicated, may hold values from -3 to 3
- chan_map: int32 [4096], replicated, may hold values from 0 to 2047
Outputs:
- mixed: bfloat16 [8, 2, 128, 4096], P(('groups', 'seq'), None, None, 'chan'), parts along dimension 0
There are 2 independent parts, one for each index of `groups`. A program takes and returns all parts, laid end to end along the dimension named above; an argument that names none is the same for every part. Nothing has to cross between parts.
All inputs are finite; a program needn't handle non-finite values.
Results may differ from a plain program's by a relative error of at most 0.0085.
Values may be sent and summed in bfloat16 or wider, within the bound.
A program may use at most 192 MiB of HBM per device.

v0:
```python
import math

import jax
import jax.numpy as jnp
import numpy as np
from jax import lax
from jax.experimental import pallas as pl
from jax.experimental.pallas import tpu as pltpu
from jax.sharding import PartitionSpec as P

HIGH = lax.Precision.HIGHEST


def shifted(x, axis, by):
    length = lax.axis_size(axis)
    pairs = [(i, i + by) for i in range(length) if 0 <= i + by < length]
    return lax.ppermute(x, axis, pairs)


def dft_tables(block_len):
    period_len = 2 * block_len
    freq_index = jnp.arange(block_len + 1, dtype=jnp.int32)[:, None]
    time_index = jnp.arange(block_len, dtype=jnp.int32)[None, :]
    angles = (freq_index * time_index % period_len).astype(jnp.float32) * (
        2.0 * math.pi / period_len
    )
    forward = jnp.concatenate([jnp.cos(angles), -jnp.sin(angles)], axis=0)
    weights = (
        jnp.where((freq_index == 0) | (freq_index == block_len), 1.0, 2.0).astype(jnp.float32)
        / period_len
    )
    inverse = jnp.concatenate(
        [(weights * jnp.cos(angles)).T, (-weights * jnp.sin(angles)).T], axis=1
    )
    sign_flip = jnp.where(freq_index[:, 0] % 2 == 0, 1.0, -1.0).astype(jnp.float32)
    return (forward, inverse, sign_flip)


def spectra_of(forward, blocks):
    freq_count = forward.shape[0] // 2
    spec = jnp.einsum("gb,hbc->hgc", forward, blocks, precision=HIGH)
    return spec.reshape(blocks.shape[0], 2, freq_count, blocks.shape[2])


def data_spectra(fwd_upper, fwd_lower, blocks):
    freq_count = fwd_upper.shape[0] // 2
    spec = jnp.einsum("gb,hbc->hgc", fwd_upper, blocks, preferred_element_type=jnp.float32)
    spec = spec + jnp.einsum("gb,hbc->hgc", fwd_lower, blocks, preferred_element_type=jnp.float32)
    return spec.reshape(blocks.shape[0], 2, freq_count, blocks.shape[2])


def accumulate(acc, spec_pair, source, own_ids, kernel_spec, total_blocks):
    src_ids = jnp.stack([source, total_blocks - 1 - source])
    lags = own_ids[:, None] - src_ids[None, :]
    valid = (lags >= 0).astype(jnp.float32)[:, :, None, None]
    picked = jnp.take(kernel_spec, jnp.clip(lags, 0, total_blocks - 1).reshape(-1), axis=0)
    picked = picked.reshape((2, 2) + kernel_spec.shape[1:])
    kern_real = picked[:, :, 0]
    kern_imag = picked[:, :, 1]
    data_real = spec_pair[None, :, 0]
    data_imag = spec_pair[None, :, 1]
    real_part = jnp.sum(valid * (kern_real * data_real - kern_imag * data_imag), axis=1)
    imag_part = jnp.sum(valid * (kern_real * data_imag + kern_imag * data_real), axis=1)
    return acc + jnp.stack([real_part, imag_part], axis=1)


def general_shards(
    tokens, w_up, w_out, rpe_in_w, rpe_in_b, rpe_mid_w, rpe_out_w, decay_rate, conv_taps, chan_map
):
    block_len = tokens.shape[2]
    chans = tokens.shape[3]
    seq_count = lax.axis_size("seq")
    seq_pos = lax.axis_index("seq")
    total_blocks = 2 * seq_count
    seq_len = total_blocks * block_len
    rim = conv_taps.shape[0] - 1
    old_count = decay_rate.shape[0]
    hidden_dim = rpe_out_w.shape[0]
    map_local = lax.dynamic_slice_in_dim(chan_map, lax.axis_index("chan") * chans, chans)
    counts = jnp.sum((map_local[:, None] == chan_map[None, :]).astype(jnp.float32), axis=1)
    one_hot = (jnp.arange(old_count, dtype=jnp.int32)[:, None] == map_local[None, :]).astype(
        jnp.float32
    )
    table = jnp.concatenate([rpe_out_w, decay_rate[None, :], conv_taps], axis=0)
    selected = jnp.dot(table, one_hot, precision=HIGH)
    out_cols = selected[:hidden_dim]
    rates = selected[hidden_dim]
    taps_local = selected[hidden_dim + 1 :]
    x_own = tokens[0]
    prev_low = shifted(tokens[:, 0, block_len - rim :], "seq", 1)[0]
    prev_high = shifted(tokens[:, 1, block_len - rim :], "seq", -1)[0]
    prev_high = jnp.where(seq_pos == seq_count - 1, x_own[0, block_len - rim :], prev_high)
    extended = jnp.stack(
        [
            jnp.concatenate([prev_low, x_own[0]], axis=0),
            jnp.concatenate([prev_high, x_own[1]], axis=0),
        ]
    ).astype(jnp.float32)
    conv = jnp.zeros((2, block_len, chans), jnp.float32)
    for shift_m in range(rim + 1):
        conv = (
            conv
            + taps_local[shift_m][None, None, :]
            * extended[:, rim - shift_m : rim - shift_m + block_len]
        )
    v_data = conv.astype(jnp.bfloat16)
    positions = jnp.arange(seq_len, dtype=jnp.int32).astype(jnp.float32)
    first = jax.nn.relu((positions / seq_len)[:, None] * rpe_in_w[None, :] + rpe_in_b[None, :])
    second = jax.nn.relu(jnp.dot(first, rpe_mid_w, precision=HIGH))
    encoded = jnp.dot(second, out_cols, precision=HIGH)
    gain = jnp.sqrt(2.0 * rates / (1.0 - jnp.exp(-2.0 * rates * seq_len)))
    kernel = encoded * jnp.exp(-rates[None, :] * positions[:, None]) * gain[None, :]
    forward, inverse, sign_flip = dft_tables(block_len)
    fwd_upper = forward.astype(jnp.bfloat16)
    fwd_lower = (forward - fwd_upper.astype(jnp.float32)).astype(jnp.bfloat16)
    half_spec = spectra_of(forward, kernel.reshape(total_blocks, block_len, chans))
    earlier = jnp.concatenate([jnp.zeros_like(half_spec[:1]), half_spec[:-1]], axis=0)
    kernel_spec = half_spec + sign_flip[None, None, :, None] * earlier
    own_ids = jnp.stack([seq_pos, total_blocks - 1 - seq_pos])
    start_acc = jnp.zeros((2, 2, block_len + 1, chans), jnp.float32)
    piece = lax.all_gather(v_data[None], "seq", axis=0, tiled=True)

    def one_source(carry, item):
        offset, blocks = item
        spec_pair = data_spectra(fwd_upper, fwd_lower, blocks)
        return (accumulate(carry, spec_pair, offset, own_ids, kernel_spec, total_blocks), None)

    offsets = jnp.arange(piece.shape[0], dtype=jnp.int32)
    result, _ = lax.scan(one_source, start_acc, (offsets, piece))
    toep = jnp.einsum(
        "tg,agc->atc", inverse, result.reshape(2, 2 * (block_len + 1), chans), precision=HIGH
    )
    up_pre = jnp.einsum(
        "qhbc,cd->qhbd",
        lax.all_gather(tokens, "chan", axis=3, tiled=True),
        w_up,
        preferred_element_type=jnp.float32,
    )
    hidden = (jax.nn.silu(up_pre) * toep[None] / counts[None, None, None, :]).astype(jnp.bfloat16)
    partial_sum = jnp.einsum("qhbc,cd->qhbd", hidden, w_out, preferred_element_type=jnp.float32)
    return lax.psum_scatter(partial_sum, "chan", scatter_dimension=3, tiled=True).astype(
        jnp.bfloat16
    )


BF = jnp.bfloat16
F32 = jnp.float32
LOW = 64


def halves(x):
    upper = x.astype(BF)
    return upper, (x - upper.astype(F32)).astype(BF)


def odd_tables(block_len):
    omega = 2.0 * np.pi * (np.arange(block_len)[:, None] + 0.5) / (2 * block_len)
    lags = np.arange(-block_len, block_len)[None, :]
    kern_table = np.concatenate([np.cos(omega * lags), -np.sin(omega * lags)], axis=0)
    data_table = kern_table[:, block_len:]
    times = np.arange(block_len)[None, :]
    back_table = np.concatenate([np.cos(omega * times), -np.sin(omega * times)], axis=0).T / block_len

    def split(table):
        table = table.astype(np.float32)
        upper = table.astype(BF)
        return upper, (table - upper.astype(np.float32)).astype(BF)

    kern_upper, kern_lower = split(kern_table)
    data_upper, data_lower = split(data_table)
    back_upper, back_lower = split(back_table)
    return (
        np.concatenate([kern_upper, kern_upper, kern_lower], axis=1),
        np.concatenate([data_upper, data_lower], axis=1),
        np.concatenate([back_upper, back_upper, back_lower], axis=1),
    )


def mm(a, b):
    return jnp.dot(a, b, preferred_element_type=F32)


def select_params(table, old_of_own, chan_map_row, hidden_dim):
    rows, old_count = table.shape
    width = old_of_own.shape[1]
    upper = table.astype(BF)
    rest = table - upper.astype(F32)
    middle = rest.astype(BF)
    lower = (rest - middle.astype(F32)).astype(BF)
    one_hot = jnp.where(
        lax.broadcasted_iota(jnp.int32, (old_count, width), 0) == old_of_own, 1.0, 0.0
    ).astype(BF)
    selected = mm(upper, one_hot) + mm(middle, one_hot) + mm(lower, one_hot)
    high_count = -(-old_count // LOW)

    def digits(ids):
        width = ids.shape[1]
        high_hot = jnp.where(
            lax.broadcasted_iota(jnp.int32, (high_count, width), 0) == (ids >> 6), 1.0, 0.0
        )
        low_hot = jnp.where(
            lax.broadcasted_iota(jnp.int32, (LOW, width), 0) == (ids & (LOW - 1)), 1.0, 0.0
        )
        return high_hot, low_hot.astype(BF)

    all_high, all_low = digits(chan_map_row)
    histogram = lax.dot_general(
        all_high.astype(BF), all_low, (((1,), (1,)), ((), ())), preferred_element_type=F32
    )
    own_high, own_low = digits(old_of_own)
    hist_upper, hist_lower = halves(histogram)
    counts = jnp.sum(own_high * (mm(hist_upper, own_low) + mm(hist_lower, own_low)), axis=0, keepdims=True)
    return selected, counts


def toep_kernel_spectra(selected, in_w, in_b, mid_w, kern_table, kspec_ref, seq_len, block_len):
    hidden_dim = mid_w.shape[0]
    width = selected.shape[1]
    rates = selected[hidden_dim : hidden_dim + 1]
    positions = lax.broadcasted_iota(jnp.int32, (seq_len, 1), 0).astype(F32)
    first = jnp.maximum((positions / seq_len) * in_w + in_b, 0.0)
    second = jnp.maximum(jnp.dot(first, mid_w, precision=HIGH, preferred_element_type=F32), 0.0)
    encoded = jnp.dot(second, selected[:hidden_dim], precision=HIGH, preferred_element_type=F32)
    gain = jnp.sqrt(2.0 * rates / (1.0 - jnp.exp(-2.0 * rates * seq_len)))
    kern = encoded * jnp.exp(-rates * positions) * gain
    upper, lower = halves(kern)
    blank = jnp.zeros((block_len, width), BF)
    upper = jnp.concatenate([blank, upper], axis=0)
    lower = jnp.concatenate([blank, lower], axis=0)
    for lag in range(seq_len // block_len):
        span = slice(lag * block_len, (lag + 2) * block_len)
        stacked = jnp.concatenate([upper[span], lower[span], upper[span]], axis=0)
        kspec_ref[lag] = mm(kern_table, stacked)


def toep_body(
    x_ref, table_ref, own_ref, map_ref, in_w_ref, in_b_ref, mid_ref, kt_ref, dt_ref, bt_ref,
    out_ref, kspec_ref, vspec_ref, acc_ref,
):
    total, block_len, width = x_ref.shape
    rim = 4
    hidden_dim = mid_ref.shape[0]
    selected, counts = select_params(table_ref[...], own_ref[...], map_ref[...], hidden_dim)
    toep_kernel_spectra(
        selected, in_w_ref[...], in_b_ref[...], mid_ref[...], kt_ref[...], kspec_ref,
        total * block_len, block_len,
    )
    taps = selected[hidden_dim + 1 : hidden_dim + 2 + rim]
    convolve_blocks(x_ref, taps, dt_ref[...], vspec_ref)
    mix_blocks(kspec_ref, vspec_ref, acc_ref, bt_ref[...], 1.0 / counts, out_ref)


def convolve_blocks(x_ref, taps, data_table, vspec_ref):
    total, block_len, width = x_ref.shape
    rim = taps.shape[0] - 1
    tail = jnp.zeros((8, width), F32)
    for block in range(total):
        own = x_ref[block].astype(F32)
        extended = jnp.concatenate([tail, own], axis=0)
        conv = taps[0:1] * own
        for shift in range(1, rim + 1):
            conv = conv + taps[shift : shift + 1] * extended[8 - shift : 8 - shift + block_len]
        tail = own[block_len - 8 :]
        v_data = conv.astype(BF)
        vspec_ref[block] = mm(data_table, jnp.concatenate([v_data, v_data], axis=0))


def mix_blocks(kspec_ref, vspec_ref, acc_ref, back_table, scale, out_ref):
    total, double_len, width = vspec_ref.shape
    block_len = double_len // 2
    rows = 32

    for block in range(total):

        def chunk(step, carry):
            start = pl.multiple_of(step * rows, rows)
            real_rows = pl.ds(start, rows)
            imag_rows = pl.ds(pl.multiple_of(start + block_len, rows), rows)
            real = jnp.zeros((rows, width), F32)
            imag = jnp.zeros((rows, width), F32)
            for source in range(block + 1):
                k_re = kspec_ref[block - source, real_rows, :]
                k_im = kspec_ref[block - source, imag_rows, :]
                v_re = vspec_ref[source, real_rows, :]
                v_im = vspec_ref[source, imag_rows, :]
                real = real + (k_re * v_re - k_im * v_im)
                imag = imag + (k_re * v_im + k_im * v_re)
            acc_ref[real_rows, :] = real
            acc_ref[imag_rows, :] = imag
            return carry

        lax.fori_loop(0, block_len // rows, chunk, 0)
        upper, lower = halves(acc_ref[...])
        toep = mm(back_table, jnp.concatenate([upper, lower, upper], axis=0))
        out_ref[block] = (toep * scale).astype(out_ref.dtype)


def shards(
    tokens, w_up, w_out, rpe_in_w, rpe_in_b, rpe_mid_w, rpe_out_w, decay_rate, conv_taps, chan_map
):
    _, _, block_len, chans = tokens.shape
    seq_count = lax.axis_size("seq")
    total = 2 * seq_count
    width = chans // seq_count
    start = lax.axis_index("chan") * chans + lax.axis_index("seq") * width
    own = lax.dynamic_slice_in_dim(chan_map, start, width)[None, :]
    table = jnp.concatenate([rpe_out_w, decay_rate[None, :], conv_taps], axis=0)
    table = jnp.concatenate([table, jnp.zeros((-table.shape[0] % 16, table.shape[1]), F32)], axis=0)
    pieces = lax.all_to_all(tokens[0], "seq", split_axis=2, concat_axis=0, tiled=True)
    pieces = pieces.reshape(seq_count, 2, block_len, width)
    ordered = jnp.concatenate([pieces[:, 0], pieces[::-1, 1]], axis=0)
    kern_table, data_table, back_table = odd_tables(block_len)
    toep = pl.pallas_call(
        toep_body,
        out_shape=jax.ShapeDtypeStruct((total, block_len, width), BF),
        in_specs=[pl.BlockSpec(memory_space=pltpu.VMEM)] * 10,
        out_specs=pl.BlockSpec(memory_space=pltpu.VMEM),
        scratch_shapes=[
            pltpu.VMEM((total, 2 * block_len, width), F32),
            pltpu.VMEM((total, 2 * block_len, width), F32),
            pltpu.VMEM((2 * block_len, width), F32),
        ],
        compiler_params=pltpu.CompilerParams(vmem_limit_bytes=48 * 1024 * 1024),
    )(
        ordered, table, own, chan_map[None, :], rpe_in_w[None, :], rpe_in_b[None, :], rpe_mid_w,
        kern_table, data_table, back_table,
    )
    returned = jnp.stack([toep[:seq_count], toep[seq_count:][::-1]], axis=1)
    returned = lax.all_to_all(returned, "seq", split_axis=0, concat_axis=3, tiled=True)[0]
    gathered = lax.all_gather(tokens[0], "chan", axis=2, tiled=True)
    up_pre = jnp.einsum("hbc,cd->hbd", gathered, w_up, preferred_element_type=F32)
    hidden = (jax.nn.silu(up_pre) * returned.astype(F32)).astype(BF)
    partial_sum = jnp.einsum("hbc,cd->hbd", hidden, w_out, preferred_element_type=F32).astype(BF)
    return lax.psum_scatter(partial_sum, "chan", scatter_dimension=2, tiled=True)[None]


def solution(mesh):
    in_specs = (
        P(("groups", "seq"), None, None, "chan"),
        P(None, "chan"),
        P("chan", None),
        P(),
        P(),
        P(),
        P(),
        P(),
        P(),
        P(),
    )
    out_specs = P(("groups", "seq"), None, None, "chan")
    def pick(*arrays):
        width = arrays[0].shape[3] // mesh.shape["seq"]
        return (general_shards if width % 128 else shards)(*arrays)

    return jax.shard_map(pick, mesh=mesh, in_specs=in_specs, out_specs=out_specs, check_vma=False)
```

profile of v0, /device:TPU:0, one launch (start us, length us, event | category | flops | bytes accessed | tf_op | source)
XLA Modules:
  0.0 113.0 jit_solution(5406800793090964084)
XLA Ops:
  6.5 0.7 all-gather.3.cloned.1.call-update
  7.3 2.0 %copy.18 = bf16[1,2,128,1024]{2,1,3,0:T(2,128)(2,1)} copy(bf16[1,2,128,1024]{3,2,1,0:T(8,128)(2,1)} %param.13) | data formatting | bytes 1048576 | tf_op args[0]
  9.3 6.3 %all-to-all-start = ((bf16[2,128,1024]{1,0,2:T(2,128)(2,1)}), bf16[2,128,1024]{1,0,2:T(2,128)(2,1)S(1)}, u32[]{:S(2)}, u32[]{:S(2)}) async-start(bf16[2,128,1024]{1,0,2:T(2,128)(2,1)} %bitcast.2), calls=%async_computation | async-start | bytes 1048576 | tf_op jit(solution)/shard_map/all_to_all | solution.py:309
  15.6 0.8 dynamic_slice.3
  16.3 0.1 pad.5.clone
  16.4 1.2 %maximum_maximum_fusion.table_ref = f32[80,2048]{1,0:T(8,128)S(1)} fusion(f32[5,2048]{1,0:T(8,128)} %param.21, f32[1,2048]{1,0:T(1,128)} %bitcast.46, f32[64,2048]{1,0:T(8,128)} %param.19, f32[80]{0:T(128)S(1)} %pad.5.clone), kind=kLoop, calls=%fused_computation.7 | loop fusion | flops 491520 | bytes 1229120 | tf_op jit(solution)/shard_map/concatenate | solution.py:308
  17.7 12.4 %all-to-all-done = bf16[2,128,1024]{1,0,2:T(2,128)(2,1)S(1)} async-done(((bf16[2,128,1024]{1,0,2:T(2,128)(2,1)}), bf16[2,128,1024]{1,0,2:T(2,128)(2,1)S(1)}, u32[]{:S(2)}, u32[]{:S(2)}) %all-to-all-start) | async-done | bytes 524320 | tf_op jit(solution)/shard_map/all_to_all | solution.py:309
  30.1 0.4 copy.20
  30.6 1.0 copy-done
  31.6 0.9 copy-done.1
  32.5 0.9 copy-done.2
  33.5 0.8 copy-done.3
  34.2 0.7 copy-done.4
  34.9 0.7 copy-done.5
  35.6 0.7 copy-done.6
  36.2 8.3 %shard_map.127 = bf16[8,128,256]{2,1,0:T(8,128)(2,1)S(1)} custom-call(bf16[8,128,256]{2,1,0:T(8,128)(2,1)S(1)} %pad_maximum_fusion.x_ref, f32[80,2048]{1,0:T(8,128)S(1)} %maximum_maximum_fusion.table_ref, s32[1,256]{1,0:T(1,128)S(1)} %bitcast.40, s32[1,4096]{1,0:T(1,128)S(1)} %bitcast.39, f32[1,64]{1,0:T(1,128)S(1)} %bitcast.41, f32[1,64]{1,0:T(1,128)S(1)} %bitcast.42, ...), custom_call_target="tpu_custom_call" | custom-call | tf_op jit(solution)/shard_map/pallas_call | solution.py:313
  44.6 0.1 pad_maximum_fusion.1
  44.7 16.4 %all_to_all.24 = bf16[4,2,128,256]{3,2,1,0:T(8,128)(2,1)S(1)} all-to-all(bf16[4,2,128,256]{3,2,1,0:T(8,128)(2,1)S(1)} %copy.21), channel_id=1, replica_groups=mesh['groups'=2,'seq'=4,'chan'=4] {'seq'}, dimensions={0} | all-to-all | bytes 1048576 | tf_op jit(solution)/shard_map/all_to_all | solution.py:329
  61.1 0.3 copy.22
  61.4 0.1 bitcast_convert_fusion
  61.5 0.3 copy.23
  61.9 6.4 %multiply_convert_fusion = bf16[2,128,1024]{2,1,0:T(8,128)(2,1)S(1)} fusion(f32[2,128,1024]{2,1,0:T(8,128)S(1)} %copy.23, bf16[4096,1024]{1,0:T(8,128)(2,1)} %param.14, bf16[1,2,128,4096]{3,2,1,0:T(8,128)(2,1)} %all-gather.3.cloned.1.call-done), kind=kOutput, calls=%fused_computation.6 | convolution fusion | flops 2149056512 | bytes 12058624 | tf_op jit(solution)/shard_map/hbc,cd->hbd/dot_general | solution.py:331
  68.3 7.1 %fusion.4 = bf16[2,128,4096]{2,1,0:T(8,128)(2,1)} fusion(bf16[2,128,1024]{2,1,0:T(8,128)(2,1)S(1)} %multiply_convert_fusion, bf16[1024,4096]{1,0:T(8,128)(2,1)} %param.15), kind=kOutput, calls=%fused_computation.4 | convolution fusion | flops 2148532224 | bytes 11010048 | tf_op jit(solution)/shard_map/hbc,cd->hbd/dot_general | solution.py:333
  75.4 30.7 %reduce-scatter.2.cloned.1.call-done = bf16[2,128,1024]{2,1,0:T(8,128)(2,1)} async-done(((bf16[2,128,4096]{2,1,0:T(8,128)(2,1)}), bf16[2,128,1024]{2,1,0:T(8,128)(2,1)}) %reduce-scatter.2.cloned.1.call-update) | async-done | bytes 524304 | tf_op jit(solution)/shard_map/reduce_scatter | solution.py:334
  (18 shorter events, 0.3 us)
Async XLA Ops:
  6.5 55.3 %all-gather.3.cloned.1.call-start = ((), (), s32[]{:S(2)}) async-start(), calls=%async_computation.4 | async-start | bytes 2621440 | tf_op jit(solution)/shard_map/all_gather | solution.py:330
  9.3 20.8 %all-to-all-start = ((bf16[2,128,1024]{1,0,2:T(2,128)(2,1)}), bf16[2,128,1024]{1,0,2:T(2,128)(2,1)S(1)}, u32[]{:S(2)}, u32[]{:S(2)}) async-start(bf16[2,128,1024]{1,0,2:T(2,128)(2,1)} %bitcast.2), calls=%async_computation | async-start | bytes 1048576 | tf_op jit(solution)/shard_map/all_to_all | solution.py:309
  15.6 90.5 %reduce-scatter.2.cloned.1.call-start = ((), (), s32[]{:S(2)}) async-start(), calls=%async_computation.3 | async-start | bytes 2621440 | tf_op jit(solution)/shard_map/reduce_scatter | solution.py:334
  30.6 1.0 copy-start
  31.6 0.9 copy-start.1
  32.5 0.9 copy-start.2
  33.5 0.8 copy-start.3
  34.2 0.7 copy-start.4
  34.9 0.7 copy-start.5
  35.6 0.7 copy-start.6
Sparse Core Ops, SparseCore 0:
  8.9 25.2 all-gather.2
  75.5 30.5 reduce-scatter.1
where the time goes:
time: 114 us; the launch traced here: 113 us
  waiting for transfers between devices  43.9 us (39%)
  blocking collectives  16.4 us (14%)
  matrix products  13.5 us (12%)
  between operations  13.5 us (12%)
  local copies, waits for them, and re-layouts  9.61 us (8%)
  Pallas kernels  8.33 us (7%)
  starting transfers between devices  6.32 us (6%)
  other arithmetic  1.41 us (1%)
    reduce_scatter x1, waiting for transfers between devices, shards(): lax.psum_scatter(partial_sum, 'chan', scatter_dimension=2, tiled=True)[None]  30.7 us
    all_to_all x1, blocking collectives, shards(): lax.all_to_all(returned, 'seq', split_axis=0, concat_axis=3, tiled=True)[0]  16.4 us
    all_to_all x1, waiting for transfers between devices, shards(): lax.all_to_all(tokens[0], 'seq', split_axis=2, concat_axis=0, tiled=True)  12.4 us
    pallas_call x1, Pallas kernels, shards(): pl.pallas_call(toep_body, out_shape=jax.ShapeDtypeStruct((total, block_le...  8.33 us
    unnamed x15, local copies, waits for them, and re-layouts  7.61 us
    dot_general x1, matrix products, shards(): jnp.einsum('hbc,cd->hbd', hidden, w_out, preferred_element_type=F32)  7.06 us
    dot_general x1, matrix products, shards(): jnp.einsum('hbc,cd->hbd', gathered, w_up, preferred_element_type=F32)  6.45 us
    all_to_all x1, starting transfers between devices, shards(): lax.all_to_all(tokens[0], 'seq', split_axis=2, concat_axis=0, tiled=True)  6.32 us
  transfers between devices with their start and end apart: 3, of which 2 were waited for; matrix products, arithmetic and copies ran while one was open for 5% of the time, Pallas kernels for 7%

commit v1 on v0

--- a/solution.py
+++ b/solution.py
@@ -1,3 +1,4 @@
+import functools
 import math
 
 import jax
@@ -233,29 +234,13 @@
         kspec_ref[lag] = mm(kern_table, stacked)
 
 
-def toep_body(
-    x_ref, table_ref, own_ref, map_ref, in_w_ref, in_b_ref, mid_ref, kt_ref, dt_ref, bt_ref,
-    out_ref, kspec_ref, vspec_ref, acc_ref,
-):
-    total, block_len, width = x_ref.shape
-    rim = 4
-    hidden_dim = mid_ref.shape[0]
-    selected, counts = select_params(table_ref[...], own_ref[...], map_ref[...], hidden_dim)
-    toep_kernel_spectra(
-        selected, in_w_ref[...], in_b_ref[...], mid_ref[...], kt_ref[...], kspec_ref,
-        total * block_len, block_len,
-    )
-    taps = selected[hidden_dim + 1 : hidden_dim + 2 + rim]
-    convolve_blocks(x_ref, taps, dt_ref[...], vspec_ref)
-    mix_blocks(kspec_ref, vspec_ref, acc_ref, bt_ref[...], 1.0 / counts, out_ref)
-
-
 def convolve_blocks(x_ref, taps, data_table, vspec_ref):
-    total, block_len, width = x_ref.shape
+    seq_count, _, block_len, width = x_ref.shape
+    total = 2 * seq_count
     rim = taps.shape[0] - 1
     tail = jnp.zeros((8, width), F32)
     for block in range(total):
-        own = x_ref[block].astype(F32)
+        own = x_ref[place_of(block, seq_count)].astype(F32)
         extended = jnp.concatenate([tail, own], axis=0)
         conv = taps[0:1] * own
         for shift in range(1, rim + 1):
@@ -265,34 +250,256 @@
         vspec_ref[block] = mm(data_table, jnp.concatenate([v_data, v_data], axis=0))
 
 
-def mix_blocks(kspec_ref, vspec_ref, acc_ref, back_table, scale, out_ref):
+def place_of(block, seq_count):
+    return (block, 0) if block < seq_count else (2 * seq_count - 1 - block, 1)
+
+
+def mix_block(block, kspec_ref, vspec_ref, acc_ref, back_table):
     total, double_len, width = vspec_ref.shape
     block_len = double_len // 2
     rows = 32
 
+    def chunk(step, carry):
+        start = pl.multiple_of(step * rows, rows)
+        real_rows = pl.ds(start, rows)
+        imag_rows = pl.ds(pl.multiple_of(start + block_len, rows), rows)
+        real = jnp.zeros((rows, width), F32)
+        imag = jnp.zeros((rows, width), F32)
+        for source in range(block + 1):
+            k_re = kspec_ref[block - source, real_rows, :]
+            k_im = kspec_ref[block - source, imag_rows, :]
+            v_re = vspec_ref[source, real_rows, :]
+            v_im = vspec_ref[source, imag_rows, :]
+            real = real + (k_re * v_re - k_im * v_im)
+            imag = imag + (k_re * v_im + k_im * v_re)
+        acc_ref[real_rows, :] = real
+        acc_ref[imag_rows, :] = imag
+        return carry
+
+    lax.fori_loop(0, block_len // rows, chunk, 0)
+    upper, lower = halves(acc_ref[...])
+    return mm(back_table, jnp.concatenate([upper, lower, upper], axis=0))
+
+
+PIECE = 256
+
+
+def layer_body(
+    seq_count, chips,
+    tokens_ref, w_up_ref, w_out_ref, rpe_out_ref, small_ref, enc_ref, map_ref, tables_ref,
+    out_ref,
+    up_w, out_w, rpe_v, small_v, enc_v, map_v, tables_v,
+    seq_x, chan_x, kspec_ref, vspec_ref, acc_ref, toep_out, toep_in, gate_ref, hidden_ref,
+    give_out, give_in, cross_out, cross_in, own_sum,
+    load_sems, xs_send, xs_recv, ag_send, ag_recv, fw_send, fw_recv, tb_send, tb_recv,
+    gv_send, gv_recv, cr_send, cr_recv,
+):
+    mesh_ids = pl.DeviceIdType.MESH
+    me = lax.axis_index("seq")
+    chan = lax.axis_index("chan")
+    chip, core = chan // 2, chan % 2
+    partner = chip * 2 + (1 - core)
+    block_len, chans = tokens_ref.shape[2], tokens_ref.shape[3]
+    width = chans // seq_count
+    total = 2 * seq_count
+    own_tokens = tokens_ref.at[0]
+
+    def remote(source, target, send, recv, device):
+        return pltpu.make_async_remote_copy(
+            src_ref=source, dst_ref=target, send_sem=send, recv_sem=recv,
+            device_id=device, device_id_type=mesh_ids,
+        )
+
+    def seq_ahead(offset):
+        return lax.rem(me + offset, seq_count)
+
+    def chip_ahead(offset):
+        return lax.rem(chip + offset, chips)
+
+    loads = [
+        pltpu.make_async_copy(source, target, load_sems.at[i])
+        for i, (source, target) in enumerate([
+            (rpe_out_ref, rpe_v), (small_ref, small_v), (enc_ref, enc_v), (map_ref, map_v),
+            (tables_ref, tables_v), (w_up_ref, up_w), (w_out_ref, out_w),
+            (own_tokens, chan_x.at[chan]),
+            (own_tokens.at[:, :, pl.ds(pl.multiple_of(me * width, width), width)], seq_x.at[me]),
+        ])
+    ]
+    for load in loads[:5]:
+        load.start()
+
+    barrier = pltpu.get_barrier_semaphore()
+    for offset in range(1, seq_count):
+        pl.semaphore_signal(barrier, inc=1, device_id={"seq": seq_ahead(offset)}, device_id_type=mesh_ids)
+    pl.semaphore_signal(barrier, inc=1, device_id={"chan": partner}, device_id_type=mesh_ids)
+    for offset in range(1, chips):
+        pl.semaphore_signal(
+            barrier, inc=1, device_id={"chan": chip_ahead(offset) * 2 + core}, device_id_type=mesh_ids
+        )
+    pl.semaphore_wait(barrier, seq_count - 1 + 1 + chips - 1)
+
+    exchange = []
+    for offset in range(1, seq_count):
+        target = seq_ahead(offset)
+        exchange.append(remote(
+            own_tokens.at[:, :, pl.ds(pl.multiple_of(target * width, width), width)], seq_x.at[me],
+            xs_send.at[offset - 1], xs_recv.at[offset - 1], {"seq": target},
+        ))
+    gather = []
+    for offset in range(1, chips):
+        gather.append(remote(
+            own_tokens, chan_x.at[chan], ag_send.at[offset], ag_recv.at[offset],
+            {"chan": chip_ahead(offset) * 2 + core},
+        ))
+    gather.append(remote(own_tokens, chan_x.at[chan], ag_send.at[0], ag_recv.at[0], {"chan": partner}))
+    for copy in exchange + gather:
+        copy.start()
+    for load in loads[5:]:
+        load.start()
+
+    for load in loads[:5]:
+        load.wait()
+    hidden_dim = rpe_v.shape[0]
+    rim = 4
+    start = pl.multiple_of(chan * chans + me * width, width)
+    table = jnp.concatenate([rpe_v[...], small_v[...]], axis=0)
+    selected, counts = select_params(table, map_v[:, pl.ds(start, width)], map_v[...], hidden_dim)
+    double_len = 2 * block_len
+    toep_kernel_spectra(
+        selected, enc_v[hidden_dim : hidden_dim + 1], enc_v[hidden_dim + 1 : hidden_dim + 2],
+        enc_v[:hidden_dim], tables_v[:double_len, : 3 * double_len], kspec_ref,
+        total * block_len, block_len,
+    )
+    taps = selected[hidden_dim + 1 : hidden_dim + 2 + rim]
+    scale = 1.0 / counts
+
+    loads[8].wait()
+    for copy in exchange:
+        copy.wait()
+    convolve_blocks(seq_x, taps, tables_v[:double_len, 3 * double_len :], vspec_ref)
+
+    forwards = []
+    for offset in range(1, chips):
+        gather[offset - 1].wait()
+        origin = lax.rem(chip + chips - offset, chips) * 2 + core
+        forward = remote(
+            chan_x.at[origin], chan_x.at[origin], fw_send.at[offset], fw_recv.at[offset], {"chan": partner}
+        )
+        forward.start()
+        forwards.append(forward)
+
+    back_table = tables_v[double_len:, : 3 * double_len]
     for block in range(total):
-
-        def chunk(step, carry):
-            start = pl.multiple_of(step * rows, rows)
-            real_rows = pl.ds(start, rows)
-            imag_rows = pl.ds(pl.multiple_of(start + block_len, rows), rows)
-            real = jnp.zeros((rows, width), F32)
-            imag = jnp.zeros((rows, width), F32)
-            for source in range(block + 1):
-                k_re = kspec_ref[block - source, real_rows, :]
-                k_im = kspec_ref[block - source, imag_rows, :]
-                v_re = vspec_ref[source, real_rows, :]
-                v_im = vspec_ref[source, imag_rows, :]
-                real = real + (k_re * v_re - k_im * v_im)
-                imag = imag + (k_re * v_im + k_im * v_re)
-            acc_ref[real_rows, :] = real
-            acc_ref[imag_rows, :] = imag
+        toep = (mix_block(block, kspec_ref, vspec_ref, acc_ref, back_table) * scale).astype(BF)
+        dest, half = place_of(block, seq_count)
+        toep_out[dest, half] = toep
+
+        @pl.when(me != dest)
+        def _():
+            remote(
+                toep_out.at[dest, half], toep_in.at[me, half], tb_send.at[dest, half],
+                tb_recv.at[me, half], {"seq": dest},
+            ).start()
+
+        @pl.when(me == dest)
+        def _():
+            toep_in[me, half] = toep
+
+    gather[-1].wait()
+    for forward in forwards:
+        forward.wait()
+    for load in loads[5:8]:
+        load.wait()
+
+    tile = PIECE
+    token_count = 2 * block_len
+
+    def gate_tile(step, carry):
+        columns = pl.ds(pl.multiple_of(step * tile, tile), tile)
+        up = jnp.zeros((token_count, tile), F32)
+        for origin in range(2 * chips):
+            up = up + mm(
+                chan_x[origin].reshape(token_count, chans), up_w[pl.ds(origin * chans, chans), columns]
+            )
+        gate_ref[:, columns] = up * jax.nn.sigmoid(up)
+        return carry
+
+    lax.fori_loop(0, chans // tile, gate_tile, 0)
+
+    for source in range(seq_count):
+
+        @pl.when(me != source)
+        def _():
+            for half in range(2):
+                remote(
+                    toep_out.at[source, half], toep_in.at[source, half], tb_send.at[source, half],
+                    tb_recv.at[source, half], {"seq": source},
+                ).wait()
+
+        columns = slice(source * width, (source + 1) * width)
+        hidden_ref[:, columns] = (
+            gate_ref[:, columns] * toep_in[source].reshape(token_count, width).astype(F32)
+        ).astype(BF)
+
+    pieces = chans // tile
+
+    def part(device, piece):
+        columns = pl.ds(pl.multiple_of(device * chans + piece * tile, tile), tile)
+        return mm(hidden_ref[...], out_w[:, columns])
+
+    def give(slot, piece):
+        return remote(
+            give_out.at[slot, piece], give_in.at[slot, piece], gv_send.at[slot, piece],
+            gv_recv.at[slot, piece], {"chan": partner},
+        )
+
+    def cross(slot, piece, offset):
+        return remote(
+            cross_out.at[slot, piece], cross_in.at[slot, piece], cr_send.at[slot, piece],
+            cr_recv.at[slot, piece], {"chan": chip_ahead(offset) * 2 + core},
+        )
+
+    def each_piece(work):
+        def step(piece, carry):
+            work(piece)
             return carry
 
-        lax.fori_loop(0, block_len // rows, chunk, 0)
-        upper, lower = halves(acc_ref[...])
-        toep = mm(back_table, jnp.concatenate([upper, lower, upper], axis=0))
-        out_ref[block] = (toep * scale).astype(out_ref.dtype)
+        lax.fori_loop(0, pieces, step, 0)
+
+    def hand_over(offset):
+        def work(piece):
+            give_out[offset, piece] = part(chip_ahead(offset) * 2 + (1 - core), piece).astype(BF)
+            give(offset, piece).start()
+
+        each_piece(work)
+
+    for offset in range(1, chips):
+        hand_over(offset)
+
+        def send_across(piece):
+            mine = part(chip_ahead(offset) * 2 + core, piece)
+            give(offset, piece).wait()
+            cross_out[offset - 1, piece] = (mine + give_in[offset, piece].astype(F32)).astype(BF)
+            cross(offset - 1, piece, offset).start()
+
+        each_piece(send_across)
+    hand_over(0)
+
+    def keep(piece):
+        own_sum[piece] = part(chan, piece)
+
+    each_piece(keep)
+
+    def finish(piece):
+        give(0, piece).wait()
+        result = own_sum[piece] + give_in[0, piece].astype(F32)
+        for offset in range(1, chips):
+            cross(offset - 1, piece, offset).wait()
+            result = result + cross_in[offset - 1, piece].astype(F32)
+        columns = pl.ds(pl.multiple_of(piece * tile, tile), tile)
+        out_ref[0, :, :, columns] = result.astype(out_ref.dtype).reshape(2, block_len, tile)
+
+    each_piece(finish)
 
 
 def shards(
@@ -300,38 +507,73 @@
 ):
     _, _, block_len, chans = tokens.shape
     seq_count = lax.axis_size("seq")
+    chan_count = lax.axis_size("chan")
+    chips = chan_count // 2
     total = 2 * seq_count
     width = chans // seq_count
-    start = lax.axis_index("chan") * chans + lax.axis_index("seq") * width
-    own = lax.dynamic_slice_in_dim(chan_map, start, width)[None, :]
-    table = jnp.concatenate([rpe_out_w, decay_rate[None, :], conv_taps], axis=0)
-    table = jnp.concatenate([table, jnp.zeros((-table.shape[0] % 16, table.shape[1]), F32)], axis=0)
-    pieces = lax.all_to_all(tokens[0], "seq", split_axis=2, concat_axis=0, tiled=True)
-    pieces = pieces.reshape(seq_count, 2, block_len, width)
-    ordered = jnp.concatenate([pieces[:, 0], pieces[::-1, 1]], axis=0)
+    double_len = 2 * block_len
+    pieces = chans // PIECE
+    hidden_dim, old_count = rpe_out_w.shape
+    small = jnp.concatenate([decay_rate[None, :], conv_taps], axis=0)
+    small = jnp.pad(small, ((0, -small.shape[0] % 16), (0, 0)))
+    encoder = jnp.concatenate([rpe_mid_w, rpe_in_w[None, :], rpe_in_b[None, :]], axis=0)
+    encoder = jnp.pad(encoder, ((0, -encoder.shape[0] % 8), (0, 0)))
     kern_table, data_table, back_table = odd_tables(block_len)
-    toep = pl.pallas_call(
-        toep_body,
-        out_shape=jax.ShapeDtypeStruct((total, block_len, width), BF),
-        in_specs=[pl.BlockSpec(memory_space=pltpu.VMEM)] * 10,
+    tables = np.concatenate(
+        [
+            np.concatenate([kern_table, data_table], axis=1),
+            np.pad(back_table, ((0, 0), (0, double_len))),
+        ],
+        axis=0,
+    )
+    token_count = 2 * block_len
+    vmem = pltpu.VMEM
+    dma = pltpu.SemaphoreType.DMA
+    return pl.pallas_call(
+        functools.partial(layer_body, seq_count, chips),
+        out_shape=jax.ShapeDtypeStruct(tokens.shape, BF),
+        in_specs=[pl.BlockSpec(memory_space=pl.ANY)] * 8,
         out_specs=pl.BlockSpec(memory_space=pltpu.VMEM),
         scratch_shapes=[
-            pltpu.VMEM((total, 2 * block_len, width), F32),
-            pltpu.VMEM((total, 2 * block_len, width), F32),
-            pltpu.VMEM((2 * block_len, width), F32),
+            vmem(w_up.shape, BF),
+            vmem(w_out.shape, BF),
+            vmem(rpe_out_w.shape, F32),
+            vmem(small.shape, F32),
+            vmem(encoder.shape, F32),
+            vmem((1, chan_map.shape[0]), jnp.int32),
+            vmem(tables.shape, BF),
+            vmem((seq_count, 2, block_len, width), BF),
+            vmem((chan_count, 2, block_len, chans), BF),
+            vmem((total, double_len, width), F32),
+            vmem((total, double_len, width), F32),
+            vmem((double_len, width), F32),
+            vmem((seq_count, 2, block_len, width), BF),
+            vmem((seq_count, 2, block_len, width), BF),
+            vmem((token_count, chans), F32),
+            vmem((token_count, chans), BF),
+            vmem((chips, pieces, token_count, PIECE), BF),
+            vmem((chips, pieces, token_count, PIECE), BF),
+            vmem((chips - 1, pieces, token_count, PIECE), BF),
+            vmem((chips - 1, pieces, token_count, PIECE), BF),
+            vmem((pieces, token_count, PIECE), F32),
+            dma((9,)),
+            dma((seq_count - 1,)),
+            dma((seq_count - 1,)),
+            dma((chips,)),
+            dma((chips,)),
+            dma((chips,)),
+            dma((chips,)),
+            dma((seq_count, 2)),
+            dma((seq_count, 2)),
+            dma((chips, pieces)),
+            dma((chips, pieces)),
+            dma((chips - 1, pieces)),
+            dma((chips - 1, pieces)),
         ],
-        compiler_params=pltpu.CompilerParams(vmem_limit_bytes=48 * 1024 * 1024),
-    )(
-        ordered, table, own, chan_map[None, :], rpe_in_w[None, :], rpe_in_b[None, :], rpe_mid_w,
-        kern_table, data_table, back_table,
-    )
-    returned = jnp.stack([toep[:seq_count], toep[seq_count:][::-1]], axis=1)
-    returned = lax.all_to_all(returned, "seq", split_axis=0, concat_axis=3, tiled=True)[0]
-    gathered = lax.all_gather(tokens[0], "chan", axis=2, tiled=True)
-    up_pre = jnp.einsum("hbc,cd->hbd", gathered, w_up, preferred_element_type=F32)
-    hidden = (jax.nn.silu(up_pre) * returned.astype(F32)).astype(BF)
-    partial_sum = jnp.einsum("hbc,cd->hbd", hidden, w_out, preferred_element_type=F32).astype(BF)
-    return lax.psum_scatter(partial_sum, "chan", scatter_dimension=2, tiled=True)[None]
+        compiler_params=pltpu.CompilerParams(
+            collective_id=0, has_side_effects=True, vmem_limit_bytes=58 * 1024 * 1024
+        ),
+    )(tokens, w_up, w_out, rpe_out_w, small, encoder, chan_map[None, :], tables)
 
 
 def solution(mesh):
@@ -349,7 +591,8 @@
     )
     out_specs = P(("groups", "seq"), None, None, "chan")
     def pick(*arrays):
-        width = arrays[0].shape[3] // mesh.shape["seq"]
-        return (general_shards if width % 128 else shards)(*arrays)
+        chans = arrays[0].shape[3]
+        narrow = (chans // mesh.shape["seq"]) % 128 or chans % PIECE or mesh.shape["chan"] < 4
+        return (general_shards if narrow else shards)(*arrays)
 
     return jax.shard_map(pick, mesh=mesh, in_specs=in_specs, out_specs=out_specs, check_vma=False)

time: 114 us -> 52.1 us (0.46)
  waiting for transfers between devices: 43.9 us -> 0 us
  Pallas kernels: 8.33 us -> 47.1 us
  blocking collectives: 16.4 us -> 0 us
  matrix products: 13.5 us -> 0 us
  between operations: 13.5 us -> 0.01 us
  local copies, waits for them, and re-layouts: 9.61 us -> 1.87 us
  starting transfers between devices: 6.32 us -> 0 us
  other arithmetic: 1.41 us -> 2.93 us
    pallas_call x1, Pallas kernels: 8.33 us -> 47.1 us  [shards(): pl.pallas_call(functools.partial(layer_body, seq_count, chips), out_shape...]
    reduce_scatter x1 -> x0, waiting for transfers between devices: 30.7 us -> none  [shards(): lax.psum_scatter(partial_sum, 'chan', scatter_dimension=2, tiled=True)[None]]
    all_to_all x1 -> x0, blocking collectives: 16.4 us -> none  [shards(): lax.all_to_all(returned, 'seq', split_axis=0, concat_axis=3, tiled=True)[0]]
    dot_general x2 -> x0, matrix products: 13.5 us -> none  [the longest x1 7.06 us: shards(): jnp.einsum('hbc,cd->hbd', hidden, w_out, preferred_element_type=F32)]
    all_to_all x1 -> x0, waiting for transfers between devices: 12.4 us -> none  [shards(): lax.all_to_all(tokens[0], 'seq', split_axis=2, concat_axis=0, tiled=True)]
    all_to_all x1 -> x0, starting transfers between devices: 6.32 us -> none  [shards(): lax.all_to_all(tokens[0], 'seq', split_axis=2, concat_axis=0, tiled=True)]
    unnamed x15 -> x1, local copies, waits for them, and re-layouts: 7.61 us -> 1.87 us
    concatenate x2, other arithmetic: 1.29 us -> 2.93 us  [the longest x1 1.52 us: shards(): small = jnp.concatenate([decay_rate[None, :], conv_taps], axis=0)]
  transfers between devices with their start and end apart: 3 -> 0, of which waited for: 2 -> 0; matrix products, arithmetic and copies ran while one was open for 5% -> 0% of each run, Pallas kernels for 7% -> 0%
where the time goes in v1:
time: 52.1 us; the launch traced here: 51.9 us
  Pallas kernels  47.1 us (90%)
  other arithmetic  2.93 us (6%)
  local copies, waits for them, and re-layouts  1.87 us (4%)
    pallas_call x1, Pallas kernels, shards(): pl.pallas_call(functools.partial(layer_body, seq_count, chips), out_shape...  47.1 us
    unnamed x1, local copies, waits for them, and re-layouts  1.87 us
    concatenate x1, other arithmetic, shards(): small = jnp.concatenate([decay_rate[None, :], conv_taps], axis=0)  1.52 us
    concatenate x1, other arithmetic, shards(): jnp.concatenate([rpe_mid_w, rpe_in_w[None, :], rpe_in_b[None, :]], axis=0)  1.41 us

profile of v1, /device:TPU:0, one launch (start us, length us, event | category | flops | bytes accessed | tf_op | source)
XLA Modules:
  0.0 51.9 jit_solution(3491704817569939077)
XLA Ops:
  0.0 1.4 %select_maximum_fusion.1.enc_ref = f32[72,64]{1,0:T(8,128)} fusion(f32[1,64]{1,0:T(1,128)} %bitcast.6, f32[1,64]{1,0:T(1,128)} %bitcast.7, f32[64,64]{1,0:T(8,128)} %param.16), kind=kLoop, calls=%fused_computation.2 | loop fusion | flops 27648 | bytes 35328 | tf_op jit(solution)/shard_map/concatenate | solution.py:519
  1.4 1.5 %select_maximum_fusion.small_ref = f32[16,2048]{1,0:T(8,128)} fusion(f32[5,2048]{1,0:T(8,128)} %param.19, f32[1,2048]{1,0:T(1,128)} %bitcast.5), kind=kLoop, calls=%fused_computation | loop fusion | flops 131072 | bytes 180224 | tf_op jit(solution)/shard_map/concatenate | solution.py:517
  2.9 47.1 %shard_map.109 = bf16[1,2,128,1024]{3,2,1,0:T(8,128)(2,1)} custom-call(bf16[1,2,128,1024]{3,2,1,0:T(8,128)(2,1)} %tokens_ref.1, bf16[4096,1024]{1,0:T(8,128)(2,1)} %w_up_ref.1, bf16[1024,4096]{1,0:T(8,128)(2,1)} %w_out_ref.1, f32[64,2048]{1,0:T(8,128)} %rpe_out_ref.1, f32[16,2048]{1,0:T(8,128)} %select_maximum_fusion.small_ref, ...), custom_call_target="tpu_custom_call" | custom-call | tf_op jit(solution)/shard_map/pallas_call | solution.py:532
  50.0 1.9 %copy.13 = bf16[1,2,128,1024]{3,2,1,0:T(8,128)(2,1)} copy(bf16[1,2,128,1024]{3,2,1,0:T(8,128)(2,1)} %shard_map.109) | data formatting | bytes 1048576

commit v2 on v1

--- a/solution.py
+++ b/solution.py
@@ -234,20 +234,21 @@
         kspec_ref[lag] = mm(kern_table, stacked)
 
 
-def convolve_blocks(x_ref, taps, data_table, vspec_ref):
+def convolve_block(block, x_ref, taps, data_table, vspec_ref):
     seq_count, _, block_len, width = x_ref.shape
-    total = 2 * seq_count
     rim = taps.shape[0] - 1
-    tail = jnp.zeros((8, width), F32)
-    for block in range(total):
-        own = x_ref[place_of(block, seq_count)].astype(F32)
-        extended = jnp.concatenate([tail, own], axis=0)
-        conv = taps[0:1] * own
-        for shift in range(1, rim + 1):
-            conv = conv + taps[shift : shift + 1] * extended[8 - shift : 8 - shift + block_len]
-        tail = own[block_len - 8 :]
-        v_data = conv.astype(BF)
-        vspec_ref[block] = mm(data_table, jnp.concatenate([v_data, v_data], axis=0))
+    own = x_ref[place_of(block, seq_count)].astype(F32)
+    if block:
+        source, half = place_of(block - 1, seq_count)
+        tail = x_ref[source, half, block_len - 16 :, :].astype(F32)[8:]
+    else:
+        tail = jnp.zeros((8, width), F32)
+    extended = jnp.concatenate([tail, own], axis=0)
+    conv = taps[0:1] * own
+    for shift in range(1, rim + 1):
+        conv = conv + taps[shift : shift + 1] * extended[8 - shift : 8 - shift + block_len]
+    v_data = conv.astype(BF)
+    vspec_ref[block] = mm(data_table, jnp.concatenate([v_data, v_data], axis=0))
 
 
 def place_of(block, seq_count):
@@ -286,9 +287,10 @@
 
 def layer_body(
     seq_count, chips,
-    tokens_ref, w_up_ref, w_out_ref, rpe_out_ref, small_ref, enc_ref, map_ref, tables_ref,
+    tokens_ref, w_up_ref, w_out_ref, rpe_out_ref, rate_ref, taps_ref, in_w_ref, in_b_ref, mid_ref,
+    map_ref, tables_ref,
     out_ref,
-    up_w, out_w, rpe_v, small_v, enc_v, map_v, tables_v,
+    up_w, out_w, rpe_v, rate_v, taps_v, in_w_v, in_b_v, mid_v, map_v, tables_v,
     seq_x, chan_x, kspec_ref, vspec_ref, acc_ref, toep_out, toep_in, gate_ref, hidden_ref,
     give_out, give_in, cross_out, cross_in, own_sum,
     load_sems, xs_send, xs_recv, ag_send, ag_recv, fw_send, fw_recv, tb_send, tb_recv,
@@ -319,13 +321,13 @@
     loads = [
         pltpu.make_async_copy(source, target, load_sems.at[i])
         for i, (source, target) in enumerate([
-            (rpe_out_ref, rpe_v), (small_ref, small_v), (enc_ref, enc_v), (map_ref, map_v),
-            (tables_ref, tables_v), (w_up_ref, up_w), (w_out_ref, out_w),
+            (rpe_out_ref, rpe_v), (rate_ref, rate_v), (taps_ref, taps_v), (in_w_ref, in_w_v),
+            (in_b_ref, in_b_v), (mid_ref, mid_v), (map_ref, map_v), (tables_ref, tables_v), (w_up_ref, up_w), (w_out_ref, out_w),
             (own_tokens, chan_x.at[chan]),
             (own_tokens.at[:, :, pl.ds(pl.multiple_of(me * width, width), width)], seq_x.at[me]),
         ])
     ]
-    for load in loads[:5]:
+    for load in loads[:8]:
         load.start()
 
     barrier = pltpu.get_barrier_semaphore()
@@ -338,125 +340,134 @@
         )
     pl.semaphore_wait(barrier, seq_count - 1 + 1 + chips - 1)
 
-    exchange = []
-    for offset in range(1, seq_count):
-        target = seq_ahead(offset)
-        exchange.append(remote(
-            own_tokens.at[:, :, pl.ds(pl.multiple_of(target * width, width), width)], seq_x.at[me],
-            xs_send.at[offset - 1], xs_recv.at[offset - 1], {"seq": target},
+    exchange, gather = ([], []), ([], [])
+    for half in range(2):
+        for offset in range(1, seq_count):
+            target = seq_ahead(offset)
+            columns = pl.ds(pl.multiple_of(target * width, width), width)
+            exchange[half].append(remote(
+                own_tokens.at[half, :, columns], seq_x.at[me, half],
+                xs_send.at[offset - 1, half], xs_recv.at[offset - 1, half], {"seq": target},
+            ))
+        for offset in range(1, chips):
+            gather[half].append(remote(
+                own_tokens.at[half], chan_x.at[chan, half], ag_send.at[offset, half],
+                ag_recv.at[offset, half], {"chan": chip_ahead(offset) * 2 + core},
+            ))
+        gather[half].append(remote(
+            own_tokens.at[half], chan_x.at[chan, half], ag_send.at[0, half], ag_recv.at[0, half],
+            {"chan": partner},
         ))
-    gather = []
-    for offset in range(1, chips):
-        gather.append(remote(
-            own_tokens, chan_x.at[chan], ag_send.at[offset], ag_recv.at[offset],
-            {"chan": chip_ahead(offset) * 2 + core},
-        ))
-    gather.append(remote(own_tokens, chan_x.at[chan], ag_send.at[0], ag_recv.at[0], {"chan": partner}))
-    for copy in exchange + gather:
-        copy.start()
-    for load in loads[5:]:
+        for copy in exchange[half] + gather[half]:
+            copy.start()
+    for load in loads[8:]:
         load.start()
 
-    for load in loads[:5]:
+    for load in loads[:8]:
         load.wait()
     hidden_dim = rpe_v.shape[0]
-    rim = 4
+    rim = taps_v.shape[0] - 1
     start = pl.multiple_of(chan * chans + me * width, width)
-    table = jnp.concatenate([rpe_v[...], small_v[...]], axis=0)
+    small = jnp.concatenate(
+        [rate_v[...], taps_v[...], jnp.zeros((16 - 2 - rim, rate_v.shape[1]), F32)], axis=0
+    )
+    table = jnp.concatenate([rpe_v[...], small], axis=0)
     selected, counts = select_params(table, map_v[:, pl.ds(start, width)], map_v[...], hidden_dim)
     double_len = 2 * block_len
     toep_kernel_spectra(
-        selected, enc_v[hidden_dim : hidden_dim + 1], enc_v[hidden_dim + 1 : hidden_dim + 2],
-        enc_v[:hidden_dim], tables_v[:double_len, : 3 * double_len], kspec_ref,
+        selected, in_w_v[...], in_b_v[...], mid_v[...], tables_v[:double_len, : 3 * double_len], kspec_ref,
         total * block_len, block_len,
     )
     taps = selected[hidden_dim + 1 : hidden_dim + 2 + rim]
     scale = 1.0 / counts
 
-    loads[8].wait()
-    for copy in exchange:
-        copy.wait()
-    convolve_blocks(seq_x, taps, tables_v[:double_len, 3 * double_len :], vspec_ref)
-
-    forwards = []
-    for offset in range(1, chips):
-        gather[offset - 1].wait()
-        origin = lax.rem(chip + chips - offset, chips) * 2 + core
-        forward = remote(
-            chan_x.at[origin], chan_x.at[origin], fw_send.at[offset], fw_recv.at[offset], {"chan": partner}
-        )
-        forward.start()
-        forwards.append(forward)
-
+    data_table = tables_v[:double_len, 3 * double_len :]
     back_table = tables_v[double_len:, : 3 * double_len]
-    for block in range(total):
+    tile = PIECE
+    pieces = chans // tile
+
+    def back(dest, half):
+        return remote(
+            toep_out.at[dest, half], toep_in.at[me, half], tb_send.at[dest, half],
+            tb_recv.at[me, half], {"seq": dest},
+        )
+
+    def receive(half):
+        for copy in exchange[half]:
+            copy.wait()
+        for block in range(half * seq_count, (half + 1) * seq_count):
+            convolve_block(block, seq_x, taps, data_table, vspec_ref)
+
+    def mix(block):
         toep = (mix_block(block, kspec_ref, vspec_ref, acc_ref, back_table) * scale).astype(BF)
         dest, half = place_of(block, seq_count)
         toep_out[dest, half] = toep
 
         @pl.when(me != dest)
         def _():
-            remote(
-                toep_out.at[dest, half], toep_in.at[me, half], tb_send.at[dest, half],
-                tb_recv.at[me, half], {"seq": dest},
-            ).start()
+            back(dest, half).start()
 
         @pl.when(me == dest)
         def _():
             toep_in[me, half] = toep
 
-    gather[-1].wait()
-    for forward in forwards:
-        forward.wait()
-    for load in loads[5:8]:
-        load.wait()
-
-    tile = PIECE
-    token_count = 2 * block_len
-
-    def gate_tile(step, carry):
-        columns = pl.ds(pl.multiple_of(step * tile, tile), tile)
-        up = jnp.zeros((token_count, tile), F32)
-        for origin in range(2 * chips):
-            up = up + mm(
-                chan_x[origin].reshape(token_count, chans), up_w[pl.ds(origin * chans, chans), columns]
-            )
-        gate_ref[:, columns] = up * jax.nn.sigmoid(up)
-        return carry
-
-    lax.fori_loop(0, chans // tile, gate_tile, 0)
-
-    for source in range(seq_count):
-
-        @pl.when(me != source)
-        def _():
-            for half in range(2):
+    def forward(offset, half):
+        origin = lax.rem(chip + chips - offset, chips) * 2 + core
+        return remote(
+            chan_x.at[origin, half], chan_x.at[origin, half], fw_send.at[offset, half],
+            fw_recv.at[offset, half], {"chan": partner},
+        )
+
+    def pass_on(half):
+        for offset in range(1, chips):
+            gather[half][offset - 1].wait()
+            forward(offset, half).start()
+
+    def gate(half):
+        gather[half][-1].wait()
+        for offset in range(1, chips):
+            forward(offset, half).wait()
+
+        def gate_tile(step, carry):
+            columns = pl.ds(pl.multiple_of(step * tile, tile), tile)
+            up = jnp.zeros((block_len, tile), F32)
+            for origin in range(2 * chips):
+                up = up + mm(chan_x[origin, half], up_w[pl.ds(origin * chans, chans), columns])
+            gate_ref[half, :, columns] = up * jax.nn.sigmoid(up)
+            return carry
+
+        lax.fori_loop(0, pieces, gate_tile, 0)
+
+    def combine(half):
+        for source in range(seq_count):
+
+            @pl.when(me != source)
+            def _():
                 remote(
                     toep_out.at[source, half], toep_in.at[source, half], tb_send.at[source, half],
                     tb_recv.at[source, half], {"seq": source},
                 ).wait()
 
-        columns = slice(source * width, (source + 1) * width)
-        hidden_ref[:, columns] = (
-            gate_ref[:, columns] * toep_in[source].reshape(token_count, width).astype(F32)
-        ).astype(BF)
-
-    pieces = chans // tile
-
-    def part(device, piece):
+            columns = slice(source * width, (source + 1) * width)
+            hidden_ref[half, :, columns] = (
+                gate_ref[half, :, columns] * toep_in[source, half].astype(F32)
+            ).astype(BF)
+
+    def part(device, half, piece):
         columns = pl.ds(pl.multiple_of(device * chans + piece * tile, tile), tile)
-        return mm(hidden_ref[...], out_w[:, columns])
-
-    def give(slot, piece):
+        return mm(hidden_ref[half], out_w[:, columns])
+
+    def give(slot, half, piece):
         return remote(
-            give_out.at[slot, piece], give_in.at[slot, piece], gv_send.at[slot, piece],
-            gv_recv.at[slot, piece], {"chan": partner},
-        )
-
-    def cross(slot, piece, offset):
+            give_out.at[half, slot, piece], give_in.at[half, slot, piece],
+            gv_send.at[half, slot, piece], gv_recv.at[half, slot, piece], {"chan": partner},
+        )
+
+    def cross(offset, half, piece):
         return remote(
-            cross_out.at[slot, piece], cross_in.at[slot, piece], cr_send.at[slot, piece],
-            cr_recv.at[slot, piece], {"chan": chip_ahead(offset) * 2 + core},
+            cross_out.at[half, offset - 1, piece], cross_in.at[half, offset - 1, piece],
+            cr_send.at[half, offset - 1, piece], cr_recv.at[half, offset - 1, piece],
+            {"chan": chip_ahead(offset) * 2 + core},
         )
 
     def each_piece(work):
@@ -466,40 +477,66 @@
 
         lax.fori_loop(0, pieces, step, 0)
 
-    def hand_over(offset):
+    def hand_over(offset, half):
         def work(piece):
-            give_out[offset, piece] = part(chip_ahead(offset) * 2 + (1 - core), piece).astype(BF)
-            give(offset, piece).start()
+            device = chip_ahead(offset) * 2 + (1 - core)
+            give_out[half, offset, piece] = part(device, half, piece).astype(BF)
+            give(offset, half, piece).start()
 
         each_piece(work)
 
-    for offset in range(1, chips):
-        hand_over(offset)
-
-        def send_across(piece):
-            mine = part(chip_ahead(offset) * 2 + core, piece)
-            give(offset, piece).wait()
-            cross_out[offset - 1, piece] = (mine + give_in[offset, piece].astype(F32)).astype(BF)
-            cross(offset - 1, piece, offset).start()
-
-        each_piece(send_across)
-    hand_over(0)
-
-    def keep(piece):
-        own_sum[piece] = part(chan, piece)
-
-    each_piece(keep)
-
-    def finish(piece):
-        give(0, piece).wait()
-        result = own_sum[piece] + give_in[0, piece].astype(F32)
+    def project(half):
         for offset in range(1, chips):
-            cross(offset - 1, piece, offset).wait()
-            result = result + cross_in[offset - 1, piece].astype(F32)
-        columns = pl.ds(pl.multiple_of(piece * tile, tile), tile)
-        out_ref[0, :, :, columns] = result.astype(out_ref.dtype).reshape(2, block_len, tile)
-
-    each_piece(finish)
+            hand_over(offset, half)
+
+            def send_across(piece):
+                mine = part(chip_ahead(offset) * 2 + core, half, piece)
+                give(offset, half, piece).wait()
+                total_of_chip = mine + give_in[half, offset, piece].astype(F32)
+                cross_out[half, offset - 1, piece] = total_of_chip.astype(BF)
+                cross(offset, half, piece).start()
+
+            each_piece(send_across)
+        hand_over(0, half)
+
+        def keep(piece):
+            own_sum[half, piece] = part(chan, half, piece)
+
+        each_piece(keep)
+
+    def finish(half):
+        def work(piece):
+            give(0, half, piece).wait()
+            result = own_sum[half, piece] + give_in[half, 0, piece].astype(F32)
+            for offset in range(1, chips):
+                cross(offset, half, piece).wait()
+                result = result + cross_in[half, offset - 1, piece].astype(F32)
+            columns = pl.ds(pl.multiple_of(piece * tile, tile), tile)
+            out_ref[0, half, :, columns] = result.astype(out_ref.dtype)
+
+        each_piece(work)
+
+    loads[11].wait()
+    receive(0)
+    for block in range(seq_count):
+        mix(block)
+    pass_on(0)
+    loads[8].wait()
+    loads[10].wait()
+    gate(0)
+    receive(1)
+    for block in range(seq_count, total):
+        mix(block)
+        if block == total - 2:
+            pass_on(1)
+    loads[9].wait()
+    combine(0)
+    project(0)
+    gate(1)
+    combine(1)
+    project(1)
+    finish(0)
+    finish(1)
 
 
 def shards(
@@ -514,10 +551,6 @@
     double_len = 2 * block_len
     pieces = chans // PIECE
     hidden_dim, old_count = rpe_out_w.shape
-    small = jnp.concatenate([decay_rate[None, :], conv_taps], axis=0)
-    small = jnp.pad(small, ((0, -small.shape[0] % 16), (0, 0)))
-    encoder = jnp.concatenate([rpe_mid_w, rpe_in_w[None, :], rpe_in_b[None, :]], axis=0)
-    encoder = jnp.pad(encoder, ((0, -encoder.shape[0] % 8), (0, 0)))
     kern_table, data_table, back_table = odd_tables(block_len)
     tables = np.concatenate(
         [
@@ -526,20 +559,22 @@
         ],
         axis=0,
     )
-    token_count = 2 * block_len
     vmem = pltpu.VMEM
     dma = pltpu.SemaphoreType.DMA
     return pl.pallas_call(
         functools.partial(layer_body, seq_count, chips),
         out_shape=jax.ShapeDtypeStruct(tokens.shape, BF),
-        in_specs=[pl.BlockSpec(memory_space=pl.ANY)] * 8,
+        in_specs=[pl.BlockSpec(memory_space=pl.ANY)] * 11,
         out_specs=pl.BlockSpec(memory_space=pltpu.VMEM),
         scratch_shapes=[
             vmem(w_up.shape, BF),
             vmem(w_out.shape, BF),
             vmem(rpe_out_w.shape, F32),
-            vmem(small.shape, F32),
-            vmem(encoder.shape, F32),
+            vmem((1, old_count), F32),
+            vmem(conv_taps.shape, F32),
+            vmem((1, hidden_dim), F32),
+            vmem((1, hidden_dim), F32),
+            vmem(rpe_mid_w.shape, F32),
             vmem((1, chan_map.shape[0]), jnp.int32),
             vmem(tables.shape, BF),
             vmem((seq_count, 2, block_len, width), BF),
@@ -549,31 +584,34 @@
             vmem((double_len, width), F32),
             vmem((seq_count, 2, block_len, width), BF),
             vmem((seq_count, 2, block_len, width), BF),
-            vmem((token_count, chans), F32),
-            vmem((token_count, chans), BF),
-            vmem((chips, pieces, token_count, PIECE), BF),
-            vmem((chips, pieces, token_count, PIECE), BF),
-            vmem((chips - 1, pieces, token_count, PIECE), BF),
-            vmem((chips - 1, pieces, token_count, PIECE), BF),
-            vmem((pieces, token_count, PIECE), F32),
-            dma((9,)),
-            dma((seq_count - 1,)),
-            dma((seq_count - 1,)),
-            dma((chips,)),
-            dma((chips,)),
-            dma((chips,)),
-            dma((chips,)),
+            vmem((2, block_len, chans), F32),
+            vmem((2, block_len, chans), BF),
+            vmem((2, chips, pieces, block_len, PIECE), BF),
+            vmem((2, chips, pieces, block_len, PIECE), BF),
+            vmem((2, chips - 1, pieces, block_len, PIECE), BF),
+            vmem((2, chips - 1, pieces, block_len, PIECE), BF),
+            vmem((2, pieces, block_len, PIECE), F32),
+            dma((12,)),
+            dma((seq_count - 1, 2)),
+            dma((seq_count - 1, 2)),
+            dma((chips, 2)),
+            dma((chips, 2)),
+            dma((chips, 2)),
+            dma((chips, 2)),
             dma((seq_count, 2)),
             dma((seq_count, 2)),
-            dma((chips, pieces)),
-            dma((chips, pieces)),
-            dma((chips - 1, pieces)),
-            dma((chips - 1, pieces)),
+            dma((2, chips, pieces)),
+            dma((2, chips, pieces)),
+            dma((2, chips - 1, pieces)),
+            dma((2, chips - 1, pieces)),
         ],
         compiler_params=pltpu.CompilerParams(
             collective_id=0, has_side_effects=True, vmem_limit_bytes=58 * 1024 * 1024
         ),
-    )(tokens, w_up, w_out, rpe_out_w, small, encoder, chan_map[None, :], tables)
+    )(
+        tokens, w_up, w_out, rpe_out_w, decay_rate[None, :], conv_taps, rpe_in_w[None, :],
+        rpe_in_b[None, :], rpe_mid_w, chan_map[None, :], tables,
+    )
 
 
 def solution(mesh):

time: 52.1 us -> 44.1 us (0.85)
  the two profiles are of different devices: /device:TPU:0 before, /device:TPU:24 now
where the time goes in v2:
time: 44.1 us; the launch traced here: 43.9 us
  Pallas kernels  42 us (95%)
  local copies, waits for them, and re-layouts  1.87 us (4%)
    pallas_call x1, Pallas kernels, shards(): pl.pallas_call(functools.partial(layer_body, seq_count, chips), out_shape...  42 us
    unnamed x1, local copies, waits for them, and re-layouts  1.87 us

profile of v2, /device:TPU:24, one launch (start us, length us, event | category | flops | bytes accessed | tf_op | source)
XLA Modules:
  0.0 43.9 jit_solution(12333867042612884320)
XLA Ops:
  0.0 42.0 %shard_map.109 = bf16[1,2,128,1024]{3,2,1,0:T(8,128)(2,1)} custom-call(bf16[1,2,128,1024]{3,2,1,0:T(8,128)(2,1)} %tokens_ref.1, bf16[4096,1024]{1,0:T(8,128)(2,1)} %w_up_ref.1, bf16[1024,4096]{1,0:T(8,128)(2,1)} %w_out_ref.1, f32[64,2048]{1,0:T(8,128)} %rpe_out_ref.1, f32[1,2048]{1,0:T(1,128)} %bitcast.5, f32[5,2048]{1,0:T(8,128)} %taps_ref.1, ...), custom_call_target="tpu_custom_call" | custom-call | tf_op jit(solution)/shard_map/pallas_call | solution.py:564
  42.0 1.9 %copy.13 = bf16[1,2,128,1024]{3,2,1,0:T(8,128)(2,1)} copy(bf16[1,2,128,1024]{3,2,1,0:T(8,128)(2,1)} %shard_map.109) | data formatting | bytes 1048576
